TPU v7x, 512 devices: a whole 4x4x16 slice. The times are simulated.
512 devices in a mesh: rows: 32 (over z_lo, x), cols: 16 (over y, z_hi, core).
Axes of the slice: x: 4, y: 4, z: 16 (z_hi: 2, z_lo: 8; z = z_hi * 8 + z_lo), core: 2. Of those that a mesh axis runs over, the one named last changes fastest.
Arguments:
- left_feat: bfloat16 [320, 32, 2048], P(None, 'rows', 'cols'), may hold values from -6 to 6
- right_feat: bfloat16 [320, 32, 2048], P(None, 'rows', 'cols'), may hold values from -6 to 6
- grad_out: bfloat16 [32, 48, 32, 2048], P(None, None, 'rows', 'cols'), may hold values from -6 to 6
- conv_weight: bfloat16 [32, 40, 3, 3, 3], replicated, may hold values from -0.21875 to 0.21875
Outputs:
- grad_left: bfloat16 [320, 32, 2048], P(None, 'rows', 'cols')
- grad_right: bfloat16 [320, 32, 2048], P(None, 'rows', 'cols')
- grad_weight: float32 [32, 40, 3, 3, 3], replicated
All inputs are finite; a program needn't handle non-finite values.
Results may differ from a plain program's by a relative error of at most 0.0029.
Values may be sent and summed in bfloat16 or wider, within the bound.
A program may use at most 64 MiB of HBM per device.

v0:
```python
import math
import jax
import jax.numpy as jnp
from jax import lax
from jax.sharding import PartitionSpec as P


def from_behind(shard, axis, by):
    count = lax.axis_size(axis)
    pairs = [(i, i + by) for i in range(count) if 0 <= i + by < count]
    return lax.ppermute(shard, axis, pairs)


def padded_2(shard, sides, width):
    for axis, dim in sides:
        count, length = (lax.axis_size(axis), shard.shape[dim])
        up = [(i, (i + 1) % count) for i in range(count - 1)]
        down = [(j, i) for i, j in up]
        last = lax.slice_in_dim(shard, length - width, length, axis=dim)
        initial = lax.slice_in_dim(shard, 0, width, axis=dim)
        before = lax.ppermute(last, axis, up)
        after = lax.ppermute(initial, axis, down)
        shard = jnp.concatenate([before, shard, after], axis=dim)
    return shard


def correlate(left_band, right_ext, levels, groups):
    channels, band_rows, tile_width = left_band.shape
    group_size = channels // groups
    left_wide = left_band.astype(jnp.float32)
    start_volume = jnp.zeros((groups, levels, band_rows, tile_width), jnp.float32)

    def correlate_one_level(level, volume):
        offset = (levels - 1 - level).astype(jnp.int32)
        shifted = lax.dynamic_slice_in_dim(right_ext, offset, tile_width, 2).astype(jnp.float32)
        product = (left_wide * shifted).reshape(groups, group_size, band_rows, tile_width)
        slab = jnp.sum(product, axis=1) * (1.0 / group_size)
        return lax.dynamic_update_slice_in_dim(volume, slab[:, None], level, 1)

    return lax.fori_loop(0, levels, correlate_one_level, start_volume)


def feature_grads(grad_volume, left_band, right_ext, levels, groups):
    channels, band_rows, tile_width = left_band.shape
    group_size = channels // groups
    left_wide = left_band.astype(jnp.float32).reshape(groups, group_size, band_rows, tile_width)
    start_left = jnp.zeros((groups, group_size, band_rows, tile_width), jnp.float32)
    start_ext = jnp.zeros((channels, band_rows, tile_width + levels - 1), jnp.float32)

    def feature_one_level(level, carry):
        grad_left, grad_ext = carry
        offset = (levels - 1 - level).astype(jnp.int32)
        shifted = lax.dynamic_slice_in_dim(right_ext, offset, tile_width, 2).astype(jnp.float32)
        slab = lax.dynamic_slice_in_dim(grad_volume, level, 1, 1)
        grad_left = grad_left + slab * shifted.reshape(groups, group_size, band_rows, tile_width)
        spread = (slab * left_wide).reshape(channels, band_rows, tile_width)
        current = lax.dynamic_slice_in_dim(grad_ext, offset, tile_width, 2)
        grad_ext = lax.dynamic_update_slice_in_dim(grad_ext, current + spread, offset, 2)
        return (grad_left, grad_ext)

    grad_left, grad_ext = lax.fori_loop(0, levels, feature_one_level, (start_left, start_ext))
    scale = 1.0 / group_size
    return (grad_left.reshape(channels, band_rows, tile_width) * scale, grad_ext * scale)


def kernel_terms(volume, padded, levels, band_rows, tile_width):
    terms = []
    for along_d in range(3):
        for along_h in range(3):
            for along_w in range(3):
                window_cut = padded[
                    :,
                    2 - along_d : 2 - along_d + levels,
                    2 - along_h : 2 - along_h + band_rows,
                    2 - along_w : 2 - along_w + tile_width,
                ]
                terms.append(
                    lax.dot_general(
                        window_cut,
                        volume,
                        (((1, 2, 3), (1, 2, 3)), ((), ())),
                        preferred_element_type=jnp.float32,
                    )
                )
    stacked = jnp.stack(terms, axis=-1)
    return stacked.reshape(stacked.shape[0], stacked.shape[1], 3, 3, 3)


def shards(left_feat, right_feat, grad_out, conv_weight):
    channels, band_rows, tile_width = left_feat.shape
    levels = grad_out.shape[1]
    groups = conv_weight.shape[1]
    margin_cols = levels - 1
    shifted_tile = from_behind(right_feat, "cols", 1)
    border = shifted_tile[:, :, tile_width - margin_cols :]
    right_ext = jnp.concatenate([border, right_feat], axis=2)
    volume = correlate(left_feat, right_ext, levels, groups).astype(jnp.bfloat16)
    padded = padded_2(grad_out, (("rows", 2), ("cols", 3)), 1)
    padded = jnp.pad(padded, ((0, 0), (1, 1), (0, 0), (0, 0)))
    flipped = jnp.transpose(jnp.flip(conv_weight, (2, 3, 4)), (1, 0, 2, 3, 4))
    layout = ("NCDHW", "OIDHW", "NCDHW")
    kernel_local = kernel_terms(volume, padded, levels, band_rows, tile_width)
    summed = lax.psum(kernel_local, ("rows", "cols"))
    grad_volume = lax.conv_general_dilated(
        padded[None],
        flipped,
        (1, 1, 1),
        "VALID",
        dimension_numbers=layout,
        preferred_element_type=jnp.float32,
    )[0]
    cells = levels * band_rows * lax.axis_size("rows") * tile_width * lax.axis_size("cols")
    grad_weight = summed * (1.0 / math.sqrt(cells))
    grad_left, grad_ext = feature_grads(grad_volume, left_feat, right_ext, levels, groups)
    own_part = grad_ext[:, :, margin_cols:]
    spill = grad_ext[:, :, :margin_cols]
    spill_tile = jnp.pad(spill, ((0, 0), (0, 0), (tile_width - margin_cols, 0)))
    arrived = from_behind(spill_tile, "cols", -1)
    grad_right = own_part + arrived
    return (grad_left.astype(jnp.bfloat16), grad_right.astype(jnp.bfloat16), grad_weight)


def solution(mesh):
    placed = (P(None, "rows", "cols"), P(None, "rows", "cols"), P(None, None, "rows", "cols"), P())
    return jax.shard_map(
        shards,
        mesh=mesh,
        in_specs=placed,
        out_specs=(P(None, "rows", "cols"), P(None, "rows", "cols"), P()),
        check_vma=False,
    )
```

profile of v0, /device:TPU:2, one launch (start us, length us, event | category | flops | bytes accessed | tf_op | source)
XLA Modules:
  0.0 600.7 jit_solution(4668678989046985764)
XLA Ops:
  8.4 3.4 collective-permute-start
  11.8 5.7 collective-permute-start.1
  21.1 46.2 %while.33 = (s32[]{:T(128)}, f32[40,48,1,128]{3,2,1,0:T(1,128)}, bf16[320,1,175]{2,0,1:T(8,128)(2,1)S(1)}, f32[320,1,128]{2,1,0:T(1,128)S(1)}, s32[]{:T(128)}, /*index=5*/s32[]{:T(128)}, s32[]{:T(128)}, s32[]{:T(128)}) while((s32[]{:T(128)}, f32[40,48,1,128]{3,2,1,0:T(1,128)}, bf16[320,1,175]{2,0,1:T(8,128)(2,1)S(1)}, ...), condition=%wide.region_4.5_spmd, body=%wide.region_2.4_spmd.sunk | while | flops 122886 | bytes 840327 | solution.py:40
  69.5 1.6 fusion.78
  71.1 2.5 copy.85
  73.6 15.5 %collective-permute-start.2 = (bf16[32,48,3,1]{1,0,3,2:T(8,128)(2,1)S(1)}, bf16[32,48,3,1]{1,0,3,2:T(8,128)(2,1)S(1)}, u32[]{:S(2)}, u32[]{:S(2)}) collective-permute-start(bf16[32,48,3,1]{1,0,3,2:T(8,128)(2,1)S(1)} %copy.85), channel_id=1, source_target_pairs={{0,1},{1,2},{2,3},{3,4},{4,5},{5,6},{6,7},{7,8},{8,9},{9,10},{10,1... | collective-permute-start | bytes 27656 | tf_op jit(solution)/shard_map/ppermute | solution.py:21
  93.1 1.9 copy.87
  95.0 9.2 %collective-permute-done.3 = bf16[32,48,3,1]{1,0,3,2:T(8,128)(2,1)S(1)} collective-permute-done((bf16[32,48,3,1]{1,0,3,2:T(8,128)(2,1)S(1)}, bf16[32,48,3,1]{1,0,3,2:T(8,128)(2,1)S(1)}, u32[]{:S(2)}, u32[]{:S(2)}) %collective-permute-start.3) | collective-permute-done | bytes 9248 | tf_op jit(solution)/shard_map/ppermute | solution.py:22
  104.2 2.9 copy.88
  107.1 2.8 fusion.16
  109.8 2.7 fusion.80
  122.9 5.7 copy.134
  128.6 4.3 pad.10.clone
  132.9 7.2 %copy.91 = bf16[32,50,3,1,8,17]{0,4,5,2,1,3:T(8,128)(2,1)} copy(bf16[32,50,3,1,8,17]{1,0,5,4,2,3:T(8,128)(2,1)} %bitcast.194) | data formatting | bytes 2611200 | tf_op jit(solution)/shard_map/conv_general_dilated | solution.py:104
  141.4 10.0 %fusion.17 = f32[48,1,8,17,40]{4,2,3,1,0:T(8,128)} fusion(bf16[32,40,3,3,3]{1,0,4,3,2:T(8,128)(2,1)S(1)} %copy-done, bf16[32,50,3,1,7,2]{0,4,5,2,1,3:T(8,128)(2,1)S(1)} %slice.141, bf16[32,50,3,1,8,17]{0,4,5,2,1,3:T(8,128)(2,1)} %copy.91, pred[8,17]{0,1:T(8,128)(4,1)S(1)} %copy-done.11), kind=kOutput, calls=%fused_computation.30 | convolution fusion | flops 455854080 | bytes 2553736 | tf_op jit(solution)/shard_map/conv_general_dilated | solution.py:104
  151.4 3.5 copy.92
  155.0 1.7 slice_bitcast_fusion
  156.7 2.5 copy.94
  159.2 109.2 %while.34 = (s32[]{:T(128)}, f32[40,8,1,128]{3,2,1,0:T(1,128)S(1)}, f32[320,1,175]{2,0,1:T(8,128)S(1)}, f32[40,48,1,128]{3,0,2,1:T(8,128)S(1)}, bf16[320,1,175]{...) while((s32[]{:T(128)}, f32[40,8,1,128]{3,2,1,0:T(1,128)S(1)}, ...), condition=%wide.region_1.2_spmd.clone, body=%wide.region_0.1_spmd.clone.sunk | while | flops 245767 | bytes 2293933 | solution.py:61
  159.4 1.6 dynamic_update_slice.25
  161.7 1.6 dynamic_update_slice.25
  164.0 1.6 dynamic_update_slice.25
  166.2 1.6 dynamic_update_slice.25
  168.5 1.6 dynamic_update_slice.25
  170.8 1.6 dynamic_update_slice.25
  173.1 1.6 dynamic_update_slice.25
  175.4 1.6 dynamic_update_slice.25
  177.6 1.6 dynamic_update_slice.25
  179.9 1.6 dynamic_update_slice.25
  182.2 1.6 dynamic_update_slice.25
  270.5 320.8 %all-reduce.4.cloned.1.call-done = f32[32,40,3,3,3]{1,0,4,3,2:T(8,128)} async-done(((f32[32,40,3,3,3]{1,0,4,3,2:T(8,128)}), f32[32,40,3,3,3]{1,0,4,3,2:T(8,128)}) %all-reduce.4.cloned.1.call-update) | async-done | bytes 138256 | tf_op jit(solution)/shard_map/psum | solution.py:103
  591.2 1.8 broadcast_multiply_fusion.1
  (644 shorter events, 159.1 us)
Async XLA Ops:
  7.2 134.3 %copy-start = (bf16[32,40,3,3,3]{1,0,4,3,2:T(8,128)(2,1)S(1)}, bf16[32,40,3,3,3]{1,0,4,3,2:T(8,128)(2,1)}, u32[]{:S(2)}) copy-start(bf16[32,40,3,3,3]{1,0,4,3,2:T(8,128)(2,1)} %param.11) | copy-start | bytes 207364
  7.2 584.1 %all-reduce.4.cloned.1.call-start = ((), (), s32[]{:S(2)}) async-start(), calls=%async_computation | async-start | bytes 884736 | tf_op jit(solution)/shard_map/psum | solution.py:103
  8.4 59.6 %collective-permute-start = (bf16[32,48,1,128]{3,0,1,2:T(8,128)(2,1)S(1)}, bf16[32,48,1,128]{3,0,1,2:T(8,128)(2,1)S(1)}, u32[]{:S(2)}, u32[]{:S(2)}) collective-permute-start(bf16[32,48,1,128]{3,0,1,2:T(8,128)(2,1)S(1)} %copy.82), channel_id=1, source_target_pairs={{0,16},{16,32},{32,48},{48,64},{64,80},{80,96},{96,112},{112,128},... | collective-permute-start | bytes 1179656 | tf_op jit(solution)/shard_map/ppermute | solution.py:21
  11.8 56.4 %collective-permute-start.1 = (bf16[32,48,1,128]{3,0,1,2:T(8,128)(2,1)S(1)}, bf16[32,48,1,128]{3,0,1,2:T(8,128)(2,1)S(1)}, u32[]{:S(2)}, u32[]{:S(2)}) collective-permute-start(bf16[32,48,1,128]{3,0,1,2:T(8,128)(2,1)S(1)} %copy.82), channel_id=1, source_target_pairs={{16,0},{32,16},{48,32},{64,48},{80,64},{96,80},{112,96},{128,112},... | collective-permute-start | bytes 1179656 | tf_op jit(solution)/shard_map/ppermute | solution.py:22
  17.5 2.4 collective-permute-start.4
  21.0 47.0 %copy-start.4 = (bf16[32,48,1,128]{3,1,2,0:T(8,128)(2,1)S(1)}, bf16[32,48,1,128]{3,1,2,0:T(8,128)(2,1)}, u32[]{:S(2)}) copy-start(bf16[32,48,1,128]{3,1,2,0:T(8,128)(2,1)} %param.10) | copy-start | bytes 1179652
  67.3 0.7 copy-start.2
  68.0 0.7 copy-start.7
  68.7 0.7 copy-start.9
  73.6 19.5 %collective-permute-start.2 = (bf16[32,48,3,1]{1,0,3,2:T(8,128)(2,1)S(1)}, bf16[32,48,3,1]{1,0,3,2:T(8,128)(2,1)S(1)}, u32[]{:S(2)}, u32[]{:S(2)}) collective-permute-start(bf16[32,48,3,1]{1,0,3,2:T(8,128)(2,1)S(1)} %copy.85), channel_id=1, source_target_pairs={{0,1},{1,2},{2,3},{3,4},{4,5},{5,6},{6,7},{7,8},{8,9},{9,10},{10,1... | collective-permute-start | bytes 27656 | tf_op jit(solution)/shard_map/ppermute | solution.py:21
  90.5 13.7 %collective-permute-start.3 = (bf16[32,48,3,1]{1,0,3,2:T(8,128)(2,1)S(1)}, bf16[32,48,3,1]{1,0,3,2:T(8,128)(2,1)S(1)}, u32[]{:S(2)}, u32[]{:S(2)}) collective-permute-start(bf16[32,48,3,1]{1,0,3,2:T(8,128)(2,1)S(1)} %copy.86), channel_id=1, source_target_pairs={{1,0},{2,1},{3,2},{4,3},{5,4},{6,5},{7,6},{8,7},{9,8},{10,9},{11,1... | collective-permute-start | bytes 27656 | tf_op jit(solution)/shard_map/ppermute | solution.py:22
  107.1 2.8 copy-start.1
  114.8 1.1 copy-start.10
  116.2 1.0 copy-start.5
  117.5 1.0 copy-start.8
  122.1 0.8 copy-start.6
  132.9 8.5 %copy-start.11 = (pred[8,17]{0,1:T(8,128)(4,1)S(1)}, pred[8,17]{0,1:T(8,128)(4,1)}, u32[]{:S(2)}) copy-start(pred[8,17]{0,1:T(8,128)(4,1)} %constant.149) | copy-start | bytes 412
  156.7 2.5 copy-start.3
  268.5 324.5 %collective-permute-start.5 = (f32[320,1,128]{2,0,1:T(8,128)S(1)}, f32[320,1,128]{2,0,1:T(8,128)S(1)}, u32[]{:S(2)}, u32[]{:S(2)}) collective-permute-start(f32[320,1,128]{2,0,1:T(8,128)S(1)} %pad.9), channel_id=1, source_target_pairs={{1,0},{2,1},{3,2},{4,3},{5,4},{6,5},{7,6},{8,7},{9,8},{10,9},{11,1... | collective-permute-start | bytes 491528 | tf_op jit(solution)/shard_map/ppermute | solution.py:11
Sparse Core Ops, SparseCore 0:
  123.0 468.2 all-reduce.3
where the time goes:
time: 602 us; the launch traced here: 601 us
  waiting for transfers between devices  330 us (55%)
  local copies, waits for them, and re-layouts  159 us (26%)
  other arithmetic  46 us (8%)
  starting transfers between devices  28.6 us (5%)
  matrix products  19.1 us (3%)
  between operations  14.3 us (2%)
    psum x1, waiting for transfers between devices, shards(): summed = lax.psum(kernel_local, ('rows', 'cols'))  321 us
    dynamic_update_slice x48, local copies, waits for them, and re-layouts, feature_one_level(): lax.dynamic_update_slice_in_dim(grad_ext, current + spread, offset, 2)  76.8 us
    dynamic_update_slice x48, local copies, waits for them, and re-layouts, correlate_one_level(): return lax.dynamic_update_slice_in_dim(volume, slab[:, None], level, 1)  29.6 us
    ppermute x2, starting transfers between devices, padded_2(): before = lax.ppermute(last, axis, up)  18.9 us
    add x48, other arithmetic, feature_one_level(): grad_left + slab * shifted.reshape(groups, group_size, band_rows, tile_wi...  16.9 us
    unnamed x29, local copies, waits for them, and re-layouts  12.7 us
  transfers between devices with their start and end apart: 7, of which 3 were waited for; matrix products, arithmetic and copies ran while one was open for 33% of the time, Pallas kernels for 0%

commit v1 on v0

--- a/solution.py
+++ b/solution.py
@@ -100,7 +100,9 @@
     flipped = jnp.transpose(jnp.flip(conv_weight, (2, 3, 4)), (1, 0, 2, 3, 4))
     layout = ("NCDHW", "OIDHW", "NCDHW")
     kernel_local = kernel_terms(volume, padded, levels, band_rows, tile_width)
-    summed = lax.psum(kernel_local, ("rows", "cols"))
+    summed = kernel_local
+    for pp in ("rows", "cols"):
+        summed = lax.psum(summed, axis_name=pp)
     grad_volume = lax.conv_general_dilated(
         padded[None],
         flipped,

time: 602 us -> 840 us (1.40)
  the two profiles are of different devices: /device:TPU:2 before, /device:TPU:1 now
where the time goes in v1:
time: 840 us; the launch traced here: 839 us
  waiting for transfers between devices  559 us (67%)
  local copies, waits for them, and re-layouts  159 us (19%)
  other arithmetic  46 us (5%)
  starting transfers between devices  38.8 us (5%)
  matrix products  19.1 us (2%)
  between operations  14.3 us (2%)
    psum x2, waiting for transfers between devices, shards(): summed = lax.psum(summed, axis_name=pp)  549 us
    dynamic_update_slice x48, local copies, waits for them, and re-layouts, feature_one_level(): lax.dynamic_update_slice_in_dim(grad_ext, current + spread, offset, 2)  76.8 us
    dynamic_update_slice x48, local copies, waits for them, and re-layouts, correlate_one_level(): return lax.dynamic_update_slice_in_dim(volume, slab[:, None], level, 1)  29.6 us
    ppermute x2, starting transfers between devices, from_behind(): return lax.ppermute(shard, axis, pairs)  18.2 us
    ppermute x2, starting transfers between devices, padded_2(): before = lax.ppermute(last, axis, up)  17 us
    add x48, other arithmetic, feature_one_level(): grad_left + slab * shifted.reshape(groups, group_size, band_rows, tile_wi...  16.9 us
  transfers between devices with their start and end apart: 8, of which 4 were waited for; matrix products, arithmetic and copies ran while one was open for 23% of the time, Pallas kernels for 0%

profile of v1, /device:TPU:1, one launch (start us, length us, event | category | flops | bytes accessed | tf_op | source)
XLA Modules:
  0.0 839.5 jit_solution(15140489160363601010)
XLA Ops:
  8.4 4.0 collective-permute-start
  13.7 16.3 %collective-permute-start.4 = (bf16[320,1,128]{2,0,1:T(8,128)(2,1)}, bf16[320,1,128]{2,0,1:T(8,128)(2,1)S(1)}, u32[]{:S(2)}, u32[]{:S(2)}) collective-permute-start(bf16[320,1,128]{2,0,1:T(8,128)(2,1)} %param.9), channel_id=1, source_target_pairs={{0,1},{1,2},{2,3},{3,4},{4,5},{5,6},{6,7},{7,8},{8,9},{9,10},{10,1... | collective-permute-start | bytes 245768 | tf_op jit(solution)/shard_map/ppermute | solution.py:11
  32.8 46.2 %while.33 = (s32[]{:T(128)}, f32[40,48,1,128]{3,2,1,0:T(1,128)}, bf16[320,1,175]{2,0,1:T(8,128)(2,1)S(1)}, f32[320,1,128]{2,1,0:T(1,128)S(1)}, s32[]{:T(128)}, /*index=5*/s32[]{:T(128)}, s32[]{:T(128)}, s32[]{:T(128)}) while((s32[]{:T(128)}, f32[40,48,1,128]{3,2,1,0:T(1,128)}, bf16[320,1,175]{2,0,1:T(8,128)(2,1)S(1)}, ...), condition=%wide.region_4.5_spmd, body=%wide.region_2.4_spmd.sunk | while | flops 122886 | bytes 840327 | solution.py:40
  81.3 1.6 fusion.78
  82.9 2.5 copy.85
  85.4 13.0 %collective-permute-start.2 = (bf16[32,48,3,1]{1,0,3,2:T(8,128)(2,1)S(1)}, bf16[32,48,3,1]{1,0,3,2:T(8,128)(2,1)S(1)}, u32[]{:S(2)}, u32[]{:S(2)}) collective-permute-start(bf16[32,48,3,1]{1,0,3,2:T(8,128)(2,1)S(1)} %copy.85), channel_id=1, source_target_pairs={{0,1},{1,2},{2,3},{3,4},{4,5},{5,6},{6,7},{7,8},{8,9},{9,10},{10,1... | collective-permute-start | bytes 27656 | tf_op jit(solution)/shard_map/ppermute | solution.py:21
  99.8 2.1 collective-permute-start.3
  103.2 1.9 copy.87
  105.1 8.5 %collective-permute-done.3 = bf16[32,48,3,1]{1,0,3,2:T(8,128)(2,1)S(1)} collective-permute-done((bf16[32,48,3,1]{1,0,3,2:T(8,128)(2,1)S(1)}, bf16[32,48,3,1]{1,0,3,2:T(8,128)(2,1)S(1)}, u32[]{:S(2)}, u32[]{:S(2)}) %collective-permute-start.3) | collective-permute-done | bytes 9248 | tf_op jit(solution)/shard_map/ppermute | solution.py:22
  113.6 2.9 copy.88
  116.5 2.7 fusion.16
  119.3 2.7 fusion.80
  132.6 5.7 copy.134
  138.3 4.3 pad.10.clone
  142.6 7.2 copy.91
  151.2 10.0 %fusion.17 = f32[48,1,8,17,40]{4,2,3,1,0:T(8,128)} fusion(bf16[32,40,3,3,3]{1,0,4,3,2:T(8,128)(2,1)S(1)} %copy-done, bf16[32,50,3,1,7,2]{0,4,5,2,1,3:T(8,128)(2,1)S(1)} %slice.141, bf16[32,50,3,1,8,17]{0,4,5,2,1,3:T(8,128)(2,1)} %copy.91, pred[8,17]{0,1:T(8,128)(4,1)S(1)} %copy-done.11), kind=kOutput, calls=%fused_computation.30 | convolution fusion | flops 455854080 | bytes 2553736 | tf_op jit(solution)/shard_map/conv_general_dilated | solution.py:106
  161.2 3.5 copy.92
  164.7 1.7 slice_bitcast_fusion
  166.4 2.5 copy.94
  168.9 109.2 %while.34 = (s32[]{:T(128)}, f32[40,8,1,128]{3,2,1,0:T(1,128)S(1)}, f32[320,1,175]{2,0,1:T(8,128)S(1)}, f32[40,48,1,128]{3,0,2,1:T(8,128)S(1)}, bf16[320,1,175]{...) while((s32[]{:T(128)}, f32[40,8,1,128]{3,2,1,0:T(1,128)S(1)}, ...), condition=%wide.region_1.2_spmd.clone, body=%wide.region_0.1_spmd.clone.sunk | while | flops 245767 | bytes 2293933 | solution.py:61
  169.1 1.6 dynamic_update_slice.25
  171.4 1.6 dynamic_update_slice.25
  173.7 1.6 dynamic_update_slice.25
  176.0 1.6 dynamic_update_slice.25
  178.2 1.6 dynamic_update_slice.25
  180.5 1.6 dynamic_update_slice.25
  182.8 1.6 dynamic_update_slice.25
  185.1 1.6 dynamic_update_slice.25
  278.2 1.9 collective-permute-start.5
  280.8 275.4 %all-reduce.5.cloned.1.call-done = f32[32,40,3,3,3]{1,0,4,3,2:T(8,128)} async-done(((f32[32,40,3,3,3]{1,0,4,3,2:T(8,128)}), f32[32,40,3,3,3]{1,0,4,3,2:T(8,128)}) %all-reduce.5.cloned.1.call-update) | async-done | bytes 138256 | tf_op jit(solution)/shard_map/psum | solution.py:105
  557.0 273.8 %all-reduce.7.cloned.1.call-done = f32[32,40,3,3,3]{1,0,4,3,2:T(8,128)} async-done(((f32[32,40,3,3,3]{1,0,4,3,2:T(8,128)}), f32[32,40,3,3,3]{1,0,4,3,2:T(8,128)}) %all-reduce.7.cloned.1.call-update) | async-done | bytes 138256 | tf_op jit(solution)/shard_map/psum | solution.py:105
  830.8 1.8 broadcast_multiply_fusion.1
  (647 shorter events, 162.3 us)
Async XLA Ops:
  7.2 144.0 %copy-start = (bf16[32,40,3,3,3]{1,0,4,3,2:T(8,128)(2,1)S(1)}, bf16[32,40,3,3,3]{1,0,4,3,2:T(8,128)(2,1)}, u32[]{:S(2)}) copy-start(bf16[32,40,3,3,3]{1,0,4,3,2:T(8,128)(2,1)} %param.11) | copy-start | bytes 207364
  7.2 549.0 %all-reduce.5.cloned.1.call-start = ((), (), s32[]{:S(2)}) async-start(), calls=%async_computation | async-start | bytes 884736 | tf_op jit(solution)/shard_map/psum | solution.py:105
  8.4 71.4 %collective-permute-start = (bf16[32,48,1,128]{3,0,1,2:T(8,128)(2,1)S(1)}, bf16[32,48,1,128]{3,0,1,2:T(8,128)(2,1)S(1)}, u32[]{:S(2)}, u32[]{:S(2)}) collective-permute-start(bf16[32,48,1,128]{3,0,1,2:T(8,128)(2,1)S(1)} %copy.82), channel_id=1, source_target_pairs={{0,16},{16,32},{32,48},{48,64},{64,80},{80,96},{96,112},{112,128},... | collective-permute-start | bytes 1179656 | tf_op jit(solution)/shard_map/ppermute | solution.py:21
  12.4 67.6 %collective-permute-start.1 = (bf16[32,48,1,128]{3,0,1,2:T(8,128)(2,1)S(1)}, bf16[32,48,1,128]{3,0,1,2:T(8,128)(2,1)S(1)}, u32[]{:S(2)}, u32[]{:S(2)}) collective-permute-start(bf16[32,48,1,128]{3,0,1,2:T(8,128)(2,1)S(1)} %copy.82), channel_id=1, source_target_pairs={{16,0},{32,16},{48,32},{64,48},{80,64},{96,80},{112,96},{128,112},... | collective-permute-start | bytes 1179656 | tf_op jit(solution)/shard_map/ppermute | solution.py:22
  13.7 18.1 %collective-permute-start.4 = (bf16[320,1,128]{2,0,1:T(8,128)(2,1)}, bf16[320,1,128]{2,0,1:T(8,128)(2,1)S(1)}, u32[]{:S(2)}, u32[]{:S(2)}) collective-permute-start(bf16[320,1,128]{2,0,1:T(8,128)(2,1)} %param.9), channel_id=1, source_target_pairs={{0,1},{1,2},{2,3},{3,4},{4,5},{5,6},{6,7},{7,8},{8,9},{9,10},{10,1... | collective-permute-start | bytes 245768 | tf_op jit(solution)/shard_map/ppermute | solution.py:11
  32.8 47.0 %copy-start.4 = (bf16[32,48,1,128]{3,1,2,0:T(8,128)(2,1)S(1)}, bf16[32,48,1,128]{3,1,2,0:T(8,128)(2,1)}, u32[]{:S(2)}) copy-start(bf16[32,48,1,128]{3,1,2,0:T(8,128)(2,1)} %param.10) | copy-start | bytes 1179652
  79.1 0.7 copy-start.2
  79.8 0.7 copy-start.7
  80.5 0.7 copy-start.9
  85.4 17.7 %collective-permute-start.2 = (bf16[32,48,3,1]{1,0,3,2:T(8,128)(2,1)S(1)}, bf16[32,48,3,1]{1,0,3,2:T(8,128)(2,1)S(1)}, u32[]{:S(2)}, u32[]{:S(2)}) collective-permute-start(bf16[32,48,3,1]{1,0,3,2:T(8,128)(2,1)S(1)} %copy.85), channel_id=1, source_target_pairs={{0,1},{1,2},{2,3},{3,4},{4,5},{5,6},{6,7},{7,8},{8,9},{9,10},{10,1... | collective-permute-start | bytes 27656 | tf_op jit(solution)/shard_map/ppermute | solution.py:21
  99.8 13.9 %collective-permute-start.3 = (bf16[32,48,3,1]{1,0,3,2:T(8,128)(2,1)S(1)}, bf16[32,48,3,1]{1,0,3,2:T(8,128)(2,1)S(1)}, u32[]{:S(2)}, u32[]{:S(2)}) collective-permute-start(bf16[32,48,3,1]{1,0,3,2:T(8,128)(2,1)S(1)} %copy.86), channel_id=1, source_target_pairs={{1,0},{2,1},{3,2},{4,3},{5,4},{6,5},{7,6},{8,7},{9,8},{10,9},{11,1... | collective-permute-start | bytes 27656 | tf_op jit(solution)/shard_map/ppermute | solution.py:22
  116.5 2.8 copy-start.1
  124.3 1.1 copy-start.10
  125.6 1.0 copy-start.5
  126.9 1.0 copy-start.8
  131.5 0.8 copy-start.6
  132.3 698.5 %all-reduce.7.cloned.1.call-start = ((), (), s32[]{:S(2)}) async-start(), calls=%async_computation.1 | async-start | bytes 884736 | tf_op jit(solution)/shard_map/psum | solution.py:105
  142.6 8.5 %copy-start.11 = (pred[8,17]{0,1:T(8,128)(4,1)S(1)}, pred[8,17]{0,1:T(8,128)(4,1)}, u32[]{:S(2)}) copy-start(pred[8,17]{0,1:T(8,128)(4,1)} %constant.149) | copy-start | bytes 412
  166.4 2.5 copy-start.3
  278.2 278.0 %collective-permute-start.5 = (f32[320,1,128]{2,0,1:T(8,128)S(1)}, f32[320,1,128]{2,0,1:T(8,128)S(1)}, u32[]{:S(2)}, u32[]{:S(2)}) collective-permute-start(f32[320,1,128]{2,0,1:T(8,128)S(1)} %pad.9), channel_id=1, source_target_pairs={{1,0},{2,1},{3,2},{4,3},{5,4},{6,5},{7,6},{8,7},{9,8},{10,9},{11,1... | collective-permute-start | bytes 491528 | tf_op jit(solution)/shard_map/ppermute | solution.py:11
Sparse Core Ops, SparseCore 0:
  132.4 423.7 all-reduce.4
  559.4 271.3 all-reduce.6
